TPU v7x, 256 devices: a whole 4x4x8 slice. The times are simulated.
256 devices in a mesh: col: 64 (over y, z, x_lo), row: 4 (over x_hi, core).
Axes of the slice: x: 4 (x_hi: 2, x_lo: 2; x = x_hi * 2 + x_lo), y: 4, z: 8, core: 2. Of those that a mesh axis runs over, the one named last changes fastest.
Arguments:
- matrix: float32 [2048, 32768], P('row', 'col'), may hold values from -0.6 to 0.6
- lower_inverses: float32 [2, 512, 512], replicated, as said below
- upper_inverses: float32 [2, 512, 512], replicated, as said below
- pivots: int32 [2, 512], replicated, may hold values from 0 to 2047, as said below
Outputs:
- factored: float32 [2048, 32768], P('row', 'col')
Inputs may be any that keep to these rules, and one draw needn't show every extreme that they name: `pivots`: in panel p, entry j is either p * 512 + j (no exchange) or a row at or beyond (p + 1) * 512; the entries of one panel that differ from p * 512 + j are distinct. `lower_inverses`: each matrix is unit lower triangular. `upper_inverses`: each matrix is upper triangular.
All inputs are finite; a program needn't handle non-finite values.
Results may differ from a plain program's by a relative error of at most 0.00011.
Values sent between devices are 32-bit elements; how exact they have to be, the bound alone decides.
A program may use at most 64 MiB of HBM per device.

v0:
```python
import jax
import jax.numpy as jnp
from jax import lax
from jax.sharding import PartitionSpec as P


def from_root(block, axis, owner):
    block = jnp.where(lax.axis_index(axis) == owner, block, jnp.zeros_like(block))
    return lax.psum(block, axis)


def row_plan(pivots, panel_step, panel_width):
    offset = panel_step * panel_width
    pivot_rows = pivots[panel_step]
    block_rows = offset + jnp.arange(panel_width, dtype=jnp.int32)
    fixed_rows = pivot_rows == block_rows
    sources = jnp.concatenate([pivot_rows, block_rows])
    targets = jnp.concatenate([block_rows, jnp.where(fixed_rows, -1, pivot_rows)])
    return (sources, targets)


def pick_rows(values, sources, row_base, local_height):
    holders = (sources >= row_base) & (sources < row_base + local_height)
    picked = jnp.take(values, jnp.clip(sources - row_base, 0, local_height - 1), axis=0)
    return jnp.where(holders[:, None], picked, 0.0)


def local(matrix, lower_inverses, upper_inverses, pivots):
    local_height, local_width = matrix.shape
    panel_count, panel_width = pivots.shape
    row_base = lax.axis_index("row") * local_height
    col_index = lax.axis_index("col")
    col_base = col_index * local_width
    local_rows = row_base + jnp.arange(local_height, dtype=jnp.int32)
    local_cols = col_base + jnp.arange(local_width, dtype=jnp.int32)
    current = matrix
    carried = None
    for panel_step in range(panel_count):
        offset = panel_step * panel_width
        sources, targets = row_plan(pivots, panel_step, panel_width)
        moved_rows = lax.psum(pick_rows(current, sources, row_base, local_height), "row")
        top_rows = moved_rows[:panel_width]
        column_mask = local_cols >= offset + panel_width
        upper_rows = jnp.dot(lower_inverses[panel_step], top_rows, precision=lax.Precision.HIGHEST)
        upper_used = jnp.where(column_mask[None, :], upper_rows, 0.0)
        new_rows = jnp.concatenate(
            [jnp.where(column_mask[None, :], upper_rows, top_rows), moved_rows[panel_width:]]
        )
        local_targets = targets - row_base
        writes = (targets >= 0) & (local_targets >= 0) & (local_targets < local_height)
        current = current.at[jnp.where(writes, local_targets, local_height)].set(
            new_rows, mode="drop"
        )
        upper_block = upper_inverses[panel_step]
        is_owner = col_index == panel_step
        own_solve = lax.cond(
            is_owner,
            lambda block: jnp.dot(block, upper_block, precision=lax.Precision.HIGHEST),
            lambda block: jnp.zeros_like(block),
            current,
        )
        lower_cols = from_root(own_solve, "col", panel_step)
        lower_mask = local_rows >= offset + panel_width
        lower_used = jnp.where(lower_mask[:, None], lower_cols, 0.0)
        carried = None
        current = current - jnp.dot(lower_used, upper_used, precision=lax.Precision.HIGHEST)
        current = jnp.where(is_owner & lower_mask[:, None], lower_cols, current)
    return current


def solution(mesh):
    return jax.shard_map(
        local,
        mesh=mesh,
        in_specs=(P("row", "col"), P(), P(), P()),
        out_specs=P("row", "col"),
        check_vma=False,
    )
```

profile of v0, /device:TPU:4, one launch (start us, length us, event | category | flops | bytes accessed | tf_op | source)
XLA Modules:
  0.0 1396.7 jit_solution(8434778153623458387)
XLA Ops:
  6.5 1.2 copy.16
  7.8 3.5 gather_fusion
  11.4 2.0 select_select_fusion.1
  13.5 64.1 %all-reduce.5.cloned.1.call-done = f32[1024,512]{1,0:T(8,128)} async-done(((f32[1024,512]{1,0:T(8,128)}), f32[1024,512]{1,0:T(8,128)}) %all-reduce.5.cloned.1.call-update) | async-done | bytes 2097168 | tf_op jit(solution)/shard_map/psum | solution.py:41
  77.5 3.6 convolution_bitcast_fusion.1
  81.1 1.3 slice_select_fusion.1
  82.4 5.5 scatter_custom_fusion
  87.9 3.1 conditional.2
  87.9 3.1 fusion
  91.0 1.1 broadcast_select_fusion.1
  92.2 604.5 %all-reduce.7.cloned.1.call-done = f32[512,512]{1,0:T(8,128)} async-done(((f32[512,512]{1,0:T(8,128)}), f32[512,512]{1,0:T(8,128)}) %all-reduce.7.cloned.1.call-update) | async-done | bytes 1048592 | tf_op jit(solution)/shard_map/psum | solution.py:9
  696.7 3.4 fusion.15
  700.1 4.9 gather_fusion.1
  705.0 3.2 select_select_fusion
  708.2 0.2 all-reduce.11.cloned.1.call-start
  708.5 58.1 %all-reduce.9.cloned.1.call-done = f32[1024,512]{1,0:T(8,128)} async-done(((f32[1024,512]{1,0:T(8,128)}), f32[1024,512]{1,0:T(8,128)}) %all-reduce.9.cloned.1.call-update) | async-done | bytes 2097168 | tf_op jit(solution)/shard_map/psum | solution.py:41
  766.6 3.6 convolution_bitcast_fusion
  770.1 1.3 slice_select_fusion
  771.4 5.5 scatter_custom_fusion.1
  776.9 0.1 conditional.3
  776.9 0.1 broadcast.223
  777.1 1.1 broadcast_select_fusion
  778.2 607.6 %all-reduce.11.cloned.1.call-done = f32[512,512]{1,0:T(8,128)} async-done(((f32[512,512]{1,0:T(8,128)}), f32[512,512]{1,0:T(8,128)}) %all-reduce.11.cloned.1.call-update) | async-done | bytes 1048592 | tf_op jit(solution)/shard_map/psum | solution.py:9
  1385.7 4.4 fusion.14
  (29 shorter events, 0.3 us)
Async XLA Ops:
  6.5 1.2 copy-start.2
  6.5 71.0 %all-reduce.5.cloned.1.call-start = ((), (), s32[]{:S(2)}) async-start(), calls=%async_computation | async-start | bytes 4194304 | tf_op jit(solution)/shard_map/psum | solution.py:41
  13.3 683.3 %all-reduce.7.cloned.1.call-start = ((), (), s32[]{:S(2)}) async-start(), calls=%async_computation.1 | async-start | bytes 2097152 | tf_op jit(solution)/shard_map/psum | solution.py:9
  77.5 3.6 copy-start
  92.1 674.5 %all-reduce.9.cloned.1.call-start = ((), (), s32[]{:S(2)}) async-start(), calls=%async_computation.2 | async-start | bytes 4194304 | tf_op jit(solution)/shard_map/psum | solution.py:41
  708.2 677.6 %all-reduce.11.cloned.1.call-start = ((), (), s32[]{:S(2)}) async-start(), calls=%async_computation.3 | async-start | bytes 2097152 | tf_op jit(solution)/shard_map/psum | solution.py:9
  766.6 3.6 copy-start.1
Sparse Core Ops, SparseCore 0:
  13.5 64.0 all-reduce.4
  92.2 604.4 all-reduce.6
  708.3 58.2 all-reduce.8
  778.3 607.4 all-reduce.10
where the time goes:
time: 1400 us
  waiting for transfers between devices  1330 us (95%)
  other arithmetic  20.9 us (1%)
  matrix products  18 us (1%)
    psum x2, waiting for transfers between devices, from_root(): return lax.psum(block, axis)  1210 us
    psum x2, waiting for transfers between devices, local(): lax.psum(pick_rows(current, sources, row_base, local_height), 'row')  122 us
  transfers between devices with their start and end apart: 4, of which 4 were waited for; matrix products, arithmetic and copies ran while one was open for 0% of the time, Pallas kernels for 0%

commit v1 on v0

v1 whole, which is shorter than its diff:
```python
import functools

import jax
import jax.numpy as jnp
from jax import lax
from jax.experimental import pallas as pl
from jax.experimental.pallas import tpu as pltpu
from jax.sharding import PartitionSpec as P

MESH = pl.DeviceIdType.MESH
PW = 512
NX, NY, NZ = 4, 4, 8
PIECE = 16
CHUNKS = 4
F32 = jnp.float32
BF16 = jnp.bfloat16


def split(value):
    high = value.astype(BF16)
    return high, (value - high.astype(F32)).astype(BF16)


def dot(a, b):
    return jnp.dot(a, b, preferred_element_type=F32)


def dot3(a, b):
    ah, al = split(a)
    bh, bl = split(b)
    return dot(ah, bh) + (dot(ah, bl) + dot(al, bh))


def device(x, y, z, core):
    return ((y * NZ + z) * 2 + lax.rem(x, 2), (x // 2) * 2 + core)


def wrap(value, size):
    return lax.rem(value + size, size)


def remote(src, dst, send, recv, target):
    return pltpu.make_async_remote_copy(
        src_ref=src, dst_ref=dst, send_sem=send, recv_sem=recv, device_id=target, device_id_type=MESH
    )


def column(row):
    shape = (PW, PW)
    eye = lax.broadcasted_iota(jnp.int32, shape, 0) == lax.broadcasted_iota(jnp.int32, shape, 1)
    return jnp.sum(jnp.where(eye, row, 0.0), axis=1, keepdims=True)


def swapped(rows, pivot_row, offset):
    lane = lax.broadcasted_iota(jnp.int32, (PW, PW), 1).astype(F32) + offset
    return rows + jnp.sum(jnp.where(pivot_row == rows, lane - rows, 0.0), axis=1, keepdims=True)


def kernel(
    a_ref, lower_ref, upper_ref, pivots_ref, o_ref,
    pan, own, acc_a, acc_b, acc_c, acc_d,
    s1_send, s1_recv, sx_send, sx_recv, sz_send, sy_send, unit_recv, swap_send, swap_recv,
    e1_send, e1_recv, e2_send, e2_recv, e3_send, e3_recv, local_sem,
):
    col = lax.axis_index("col")
    row = lax.axis_index("row")
    core = lax.rem(row, 2)
    xh = row // 2
    x = xh * 2 + lax.rem(col, 2)
    y = col // (2 * NZ)
    z = lax.rem(col // 2, NZ)
    root = (y == 0) & (z == 0)
    mate = device(x, y, z, 1 - core)
    x_far = device(wrap(x + 2, NX), y, z, core)

    partners = [mate]
    partners += [device(wrap(x + d, NX), y, z, core) for d in (1, 2, 3)]
    partners += [device(x, wrap(y + d, NY), z, core) for d in (1, 2, 3)]
    partners += [device(x, y, wrap(z + d, NZ), core) for d in (1, -1)]
    barrier = pltpu.get_barrier_semaphore()
    for partner in partners:
        pl.semaphore_signal(barrier, inc=1, device_id=partner, device_id_type=MESH)

    @pl.when(jnp.logical_not(root))
    def _():
        pl.semaphore_signal(barrier, inc=1, device_id=device(x, 0, 0, core), device_id_type=MESH)
        pl.semaphore_wait(barrier, len(partners))

    @pl.when(root)
    def _():
        pl.semaphore_wait(barrier, len(partners) + NY * NZ - 1)

    def run(c):
        def start_row(yy, zz):
            return pl.multiple_of(PIECE * (yy * NZ + zz if c == 0 else zz * NY + yy), PIECE)

        def unit(yy, zz):
            return pan.at[c, :, pl.ds(start_row(yy, zz), PIECE), :]

        def piece(xx, yy, zz):
            return pan.at[c, xx, pl.ds(start_row(yy, zz), PIECE), :]

        def unit_sem(yy, zz):
            return unit_recv.at[yy * NZ + zz]

        @pl.when(root)
        def _():
            def send_piece(i, carry):
                yy = i // NZ
                zz = lax.rem(i, NZ)
                remote(
                    a_ref.at[pl.ds(start_row(yy, zz), PIECE), :], piece(x, yy, zz),
                    s1_send, s1_recv, device(x, yy, zz, c),
                ).start()
                return carry

            lax.fori_loop(1, NY * NZ, send_piece, 0)
            mine = pltpu.make_async_copy(
                a_ref.at[pl.ds(start_row(0, 0), PIECE), :], piece(x, 0, 0), local_sem
            )
            mine.start()
            mine.wait()

        chunk = PW // CHUNKS
        base = row * PW
        far_base = (wrap(xh + 1, 2) * 2 + c) * PW
        for i in range(CHUNKS):
            remote(
                a_ref.at[pl.ds(i * chunk, chunk), :],
                own.at[pl.ds(base + i * chunk, chunk), :],
                e1_send, e1_recv.at[i], x_far,
            ).start()
        remote(a_ref, own.at[pl.ds(base, PW), :], e2_send, e2_recv, mate).start()
        keep = pltpu.make_async_copy(a_ref, own.at[pl.ds(base, PW), :], local_sem)
        keep.start()
        keep.wait()

        def pass_far(i):
            rows = own.at[pl.ds(far_base + i * chunk, chunk), :]
            remote(rows, rows, e1_send, e1_recv.at[i], x_far).wait_recv()
            remote(rows, rows, e3_send, e3_recv, mate).start()

        @pl.when(jnp.logical_not(root))
        def _():
            remote(piece(x, y, z), piece(x, y, z), s1_send, s1_recv, mate).wait_recv()

        for d in (1, 2, 3):
            remote(
                piece(x, y, z), piece(x, y, z), sx_send, sx_recv.at[d - 1],
                device(wrap(x + d, NX), y, z, c),
            ).start()
        for d in (1, 2, 3):
            got = piece(wrap(x - d, NX), y, z)
            remote(got, got, sx_send, sx_recv.at[d - 1], mate).wait_recv()

        def send_z(yy, zz, d):
            remote(
                unit(yy, zz), unit(yy, zz), sz_send, unit_sem(yy, zz), device(x, y, wrap(z + d, NZ), c)
            ).start()

        def send_y(yy, zz):
            for d in (1, 3, 2):
                remote(
                    unit(yy, zz), unit(yy, zz), sy_send, unit_sem(yy, zz),
                    device(x, wrap(y + d, NY), z, c),
                ).start()

        def send_mate(yy, zz):
            remote(unit(yy, zz), unit(yy, zz), swap_send, swap_recv, mate).start()

        def arrived(yy, zz):
            remote(unit(yy, zz), unit(yy, zz), sz_send, unit_sem(yy, zz), mate).wait_recv()

        if c == 0:
            send_z(y, z, 1)
            send_z(y, z, -1)
            send_y(y, z)
            send_mate(y, z)
            late = [z]
            for s in (1, 2, 3, 4):
                now = []
                zz = wrap(z - s, NZ)
                arrived(y, zz)
                if s < 4:
                    send_z(y, zz, 1)
                send_y(y, zz)
                send_mate(y, zz)
                now.append(zz)
                if s < 4:
                    zz = wrap(z + s, NZ)
                    arrived(y, zz)
                    if s < 3:
                        send_z(y, zz, -1)
                    send_y(y, zz)
                    send_mate(y, zz)
                    now.append(zz)
                for zz in late:
                    for d in (1, 3, 2):
                        yy = wrap(y - d, NY)
                        arrived(yy, zz)
                        send_mate(yy, zz)
                late = now
                pass_far(s - 1)
            for zz in late:
                for d in (1, 3, 2):
                    yy = wrap(y - d, NY)
                    arrived(yy, zz)
                    send_mate(yy, zz)
            z_units, y_units = 7, 24
        else:
            send_y(y, z)
            order = [y] + [wrap(y + d, NY) for d in (1, 3, 2)]
            for yy in order:
                if yy is not y:
                    arrived(yy, z)
                send_z(yy, z, 1)
                send_z(yy, z, -1)
                send_mate(yy, z)
            for s in (1, 2, 3, 4):
                for yy in order:
                    zz = wrap(z - s, NZ)
                    arrived(yy, zz)
                    if s < 4:
                        send_z(yy, zz, 1)
                    send_mate(yy, zz)
                    if s < 4:
                        zz = wrap(z + s, NZ)
                        arrived(yy, zz)
                        if s < 3:
                            send_z(yy, zz, -1)
                        send_mate(yy, zz)
                pass_far(s - 1)
            z_units, y_units = 28, 3

        def whole(send, recv, ref):
            return remote(ref, ref, send, recv, mate)

        whole(sz_send, swap_recv, pan.at[c, :, pl.ds(0, PIECE * z_units), :]).wait_send()
        whole(sy_send, swap_recv, pan.at[c, :, pl.ds(0, PIECE * y_units), :]).wait_send()
        whole(sx_send, swap_recv, pan.at[c, pl.ds(0, 3), pl.ds(0, PIECE), :]).wait_send()
        whole(swap_send, swap_recv, pan.at[c]).wait_send()
        whole(swap_send, swap_recv, pan.at[1 - c]).wait_recv()
        block = own.at[pl.ds(0, PW), :]
        whole(e1_send, e3_recv, block).wait_send()
        whole(e2_send, e2_recv, block).wait()
        whole(e3_send, e3_recv, block).wait()

        @pl.when(root)
        def _():
            rest = pan.at[c, 0, pl.ds(0, PIECE * (NY * NZ - 1)), :]
            whole(s1_send, swap_recv, rest).wait_send()

    for c in (0, 1):
        pl.when(core == c)(functools.partial(run, c))

    first = pivots_ref[0:1, :].astype(F32)
    second = pivots_ref[1:2, :].astype(F32)
    src0 = column(first)
    src1 = swapped(column(second), first, 0.0)
    place = lax.broadcasted_iota(jnp.int32, (PW, 1), 0) + row * PW
    srcr = swapped(swapped(place.astype(F32), second, float(PW)), first, 0.0)

    lane = lax.broadcasted_iota(jnp.int32, (PW, PW), 1)

    def one_hot(src, q):
        return jnp.where((lane + q * PW).astype(F32) == src, 1.0, 0.0).astype(BF16)

    def take(src, load, dst):
        dst[...] = jnp.zeros((PW, PW), F32)

        def step(q, carry):
            high, low = split(load(q))
            pick = one_hot(src, q)
            dst[...] += dot(pick, high) + dot(pick, low)
            return carry

        lax.fori_loop(0, 4, step, 0)

    def own_block(q):
        return own[pl.ds(pl.multiple_of(q * PW, PW), PW), :]

    def panel_block(b):
        return lambda q: pan[lax.rem(q, 2), (q // 2) * 2 + b]

    take(src0, own_block, acc_a)

    @pl.when((row == 0) & (col == 0))
    def _():
        o_ref[...] = acc_a[...]

    @pl.when(jnp.logical_not((row == 0) & (col == 0)))
    def _():
        acc_a[...] = dot3(lower_ref[0], acc_a[...])

    @pl.when((row == 0) & (col > 0))
    def _():
        o_ref[...] = acc_a[...]

    @pl.when(row > 0)
    def _():
        take(src1, panel_block(0), acc_b)
        acc_b[...] = dot3(acc_b[...], upper_ref[0])

        @pl.when((row == 1) & (col == 0))
        def _():
            o_ref[...] = acc_b[...]

        @pl.when(jnp.logical_not((row == 1) & (col == 0)))
        def _():
            take(src1, own_block, acc_c)
            acc_c[...] = acc_c[...] - dot3(acc_b[...], acc_a[...])

        @pl.when((row == 1) & (col == 1))
        def _():
            o_ref[...] = acc_c[...]

        @pl.when((row > 1) | (col > 1))
        def _():
            acc_c[...] = dot3(lower_ref[1], acc_c[...])

        @pl.when((row == 1) & (col > 1))
        def _():
            o_ref[...] = acc_c[...]

    @pl.when(row > 1)
    def _():
        take(srcr, panel_block(0), acc_b)
        acc_b[...] = dot3(acc_b[...], upper_ref[0])

        @pl.when(col == 0)
        def _():
            o_ref[...] = acc_b[...]

        @pl.when(col > 0)
        def _():
            take(src0, panel_block(1), acc_d)
            acc_d[...] = dot3(lower_ref[0], acc_d[...])
            o_ref[...] = dot3(acc_b[...], acc_d[...])
            take(srcr, panel_block(1), acc_d)
            acc_d[...] = dot3(acc_d[...] - o_ref[...], upper_ref[1])

        @pl.when(col == 1)
        def _():
            o_ref[...] = acc_d[...]

        @pl.when(col > 1)
        def _():
            take(srcr, own_block, o_ref)
            o_ref[...] = o_ref[...] - dot3(acc_b[...], acc_a[...]) - dot3(acc_d[...], acc_c[...])


def local(matrix, lower_inverses, upper_inverses, pivots):
    vmem = pl.BlockSpec(memory_space=pltpu.VMEM)
    dma = pltpu.SemaphoreType.DMA
    block = pltpu.VMEM((PW, PW), F32)
    return pl.pallas_call(
        kernel,
        out_shape=jax.ShapeDtypeStruct((PW, PW), F32),
        in_specs=[pl.BlockSpec(memory_space=pl.ANY), vmem, vmem, vmem],
        out_specs=vmem,
        scratch_shapes=[
            pltpu.VMEM((2, NX, PW, PW), F32),
            pltpu.VMEM((4 * PW, PW), F32),
            block, block, block, block,
            dma, dma, dma, dma((3,)), dma, dma, dma((NY * NZ,)), dma, dma,
            dma, dma((CHUNKS,)), dma, dma, dma, dma, dma,
        ],
        compiler_params=pltpu.CompilerParams(
            collective_id=0, has_side_effects=True, vmem_limit_bytes=56 * 2**20
        ),
        name="panels",
    )(matrix, lower_inverses, upper_inverses, pivots)


def solution(mesh):
    return jax.shard_map(
        local,
        mesh=mesh,
        in_specs=(P("row", "col"), P(), P(), P()),
        out_specs=P("row", "col"),
        check_vma=False,
    )
```

time: 1400 us -> 107 us (0.08)
  the two profiles are of different devices: /device:TPU:4 before, /device:TPU:63 now
where the time goes in v1:
time: 107 us
  Pallas kernels  105 us (98%)
  local copies, waits for them, and re-layouts  2.26 us (2%)
    pallas_call x1, Pallas kernels, local(): pl.pallas_call(kernel, out_shape=jax.ShapeDtypeStruct((PW, PW), F32), in_...  105 us
    unnamed x1, local copies, waits for them, and re-layouts  2.26 us

profile of v1, /device:TPU:63, one launch (start us, length us, event | category | flops | bytes accessed | tf_op | source)
XLA Modules:
  0.0 107.2 jit_solution(16958023438862255108)
XLA Ops:
  0.0 104.9 %panels.1 = f32[512,512]{1,0:T(8,128)} custom-call(f32[512,512]{1,0:T(8,128)} %a_ref.1, f32[2,512,512]{2,1,0:T(8,128)} %lower_ref.1, f32[2,512,512]{2,1,0:T(8,128)} %upper_ref.1, s32[2,512]{1,0:T(2,128)} %pivots_ref.1), custom_call_target="tpu_custom_call" | custom-call | tf_op jit(solution)/shard_map/panels/pallas_call | solution.py:356
  104.9 2.3 %copy.6 = f32[512,512]{1,0:T(8,128)} copy(f32[512,512]{1,0:T(8,128)} %panels.1) | data formatting | bytes 2097152

commit v2 on v1

v2 whole, which is shorter than its diff:
```python
import functools

import jax
import jax.numpy as jnp
from jax import lax
from jax.experimental import pallas as pl
from jax.experimental.pallas import tpu as pltpu
from jax.sharding import PartitionSpec as P

MESH = pl.DeviceIdType.MESH
PW = 512
NX, NY, NZ = 4, 4, 8
PIECE = 16
CHUNKS = 4
LANES = 128
OWN_0, OWN_1, OWN_R, PANEL_0_1, PANEL_0_R, PANEL_1_0, PANEL_1_R = range(7)
F32 = jnp.float32
BF16 = jnp.bfloat16


def split(value):
    high = value.astype(BF16)
    return high, (value - high.astype(F32)).astype(BF16)


def dot(a, b):
    return jnp.dot(a, b, preferred_element_type=F32)


def dot3(a, b):
    return dot(a[0], b[0]) + (dot(a[0], b[1]) + dot(a[1], b[0]))


def device(x, y, z, core):
    return ((y * NZ + z) * 2 + lax.rem(x, 2), (x // 2) * 2 + core)


def wrap(value, size):
    return lax.rem(value + size, size)


def remote(src, dst, send, recv, target):
    return pltpu.make_async_remote_copy(
        src_ref=src, dst_ref=dst, send_sem=send, recv_sem=recv, device_id=target, device_id_type=MESH
    )


def column(row):
    shape = (PW, PW)
    eye = lax.broadcasted_iota(jnp.int32, shape, 0) == lax.broadcasted_iota(jnp.int32, shape, 1)
    return jnp.sum(jnp.where(eye, row, 0.0), axis=1, keepdims=True)


def swapped(rows, pivot_row, offset):
    lane = lax.broadcasted_iota(jnp.int32, (PW, PW), 1).astype(F32) + offset
    return rows + jnp.sum(jnp.where(pivot_row == rows, lane - rows, 0.0), axis=1, keepdims=True)


def kernel(
    a_ref, lower_ref, upper_ref, pivots_ref, o_ref,
    pan, own, acc, inverses, high_parts, low_parts, src,
    s1_send, s1_recv, sx_send, sx_recv, sz_send, sy_send, unit_recv, swap_send, swap_recv,
    e1_send, e1_recv, e2_send, e2_recv, e3_send, e3_recv, local_sem, keep_sem, inverse_sem,
):
    col = lax.axis_index("col")
    row = lax.axis_index("row")
    core = lax.rem(row, 2)
    xh = row // 2
    x = xh * 2 + lax.rem(col, 2)
    y = col // (2 * NZ)
    z = lax.rem(col // 2, NZ)
    root = (y == 0) & (z == 0)
    mate = device(x, y, z, 1 - core)
    x_far = device(wrap(x + 2, NX), y, z, core)

    partners = [mate]
    partners += [device(wrap(x + d, NX), y, z, core) for d in (1, 2, 3)]
    partners += [device(x, wrap(y + d, NY), z, core) for d in (1, 2, 3)]
    partners += [device(x, y, wrap(z + d, NZ), core) for d in (1, -1)]
    barrier = pltpu.get_barrier_semaphore()
    for partner in partners:
        pl.semaphore_signal(barrier, inc=1, device_id=partner, device_id_type=MESH)

    @pl.when(jnp.logical_not(root))
    def _():
        pl.semaphore_signal(barrier, inc=1, device_id=device(x, 0, 0, core), device_id_type=MESH)

    loads = [
        pltpu.make_async_copy(lower_ref, inverses.at[0], inverse_sem.at[0]),
        pltpu.make_async_copy(upper_ref, inverses.at[1], inverse_sem.at[1]),
    ]
    for load in loads:
        load.start()

    first = pivots_ref[0:1, :].astype(F32)
    second = pivots_ref[1:2, :].astype(F32)
    place = (lax.broadcasted_iota(jnp.int32, (PW, 1), 0) + row * PW).astype(F32)
    src[0] = jnp.broadcast_to(column(first), (PW, LANES))
    src[1] = jnp.broadcast_to(swapped(column(second), first, 0.0), (PW, LANES))
    src[2] = jnp.broadcast_to(swapped(swapped(place, second, float(PW)), first, 0.0), (PW, LANES))
    acc[...] = jnp.zeros(acc.shape, F32)

    @pl.when(jnp.logical_not(root))
    def _():
        pl.semaphore_wait(barrier, len(partners))

    @pl.when(root)
    def _():
        pl.semaphore_wait(barrier, len(partners) + NY * NZ - 1)

    lane = lax.broadcasted_iota(jnp.int32, (1, LANES), 1)

    def take(values, ids, targets):
        high, low = split(values)
        for which, dst in targets:
            pick = jnp.concatenate(
                [jnp.where(src[which] == part.astype(F32), 1.0, 0.0).astype(BF16) for part in ids], axis=1
            )
            acc[dst] += dot(pick, high) + dot(pick, low)

    def own_item(half, i):
        start = half * 2 * PW + i * LANES
        starts = [pl.multiple_of(start + j * PW, LANES) for j in (0, 1)]
        values = jnp.concatenate([own[pl.ds(at, LANES), :] for at in starts], axis=0)
        take(values, [lane + at for at in starts], [(0, OWN_0), (1, OWN_1), (2, OWN_R)])

    def panel_item(zz, b):
        rows = [pl.multiple_of(yy * LANES + zz * PIECE, PIECE) for yy in range(NY)]
        parts = [pan[0, 2 * q + b, pl.ds(at, PIECE), :] for q in (0, 1) for at in rows]
        at = pl.multiple_of(zz * 64, 64)
        parts += [pan[1, 2 * q + b, pl.ds(at, 64), :] for q in (0, 1)]
        within = lax.rem(lane, 64)
        high = (lane // 64) * (2 * PW)
        ids = [
            high + (within // PIECE) * LANES + lax.rem(within, PIECE) + zz * PIECE,
            high + PW + within + zz * 64,
        ]
        targets = [(2, PANEL_0_R), (1, PANEL_0_1)] if b == 0 else [(2, PANEL_1_R), (0, PANEL_1_0)]
        take(jnp.concatenate(parts, axis=0), ids, targets)

    def level(s):
        return [z] if s == 0 else [wrap(z + 4, NZ)] if s == 4 else [wrap(z - s, NZ), wrap(z + s, NZ)]

    def run(c):
        def start_row(yy, zz):
            return pl.multiple_of(PIECE * (yy * NZ + zz if c == 0 else zz * NY + yy), PIECE)

        def unit(yy, zz):
            return pan.at[c, :, pl.ds(start_row(yy, zz), PIECE), :]

        def half_unit(yy, zz, h):
            return pan.at[c, pl.ds(2 * h, 2), pl.ds(start_row(yy, zz), PIECE), :]

        def piece(xx, yy, zz):
            return pan.at[c, xx, pl.ds(start_row(yy, zz), PIECE), :]

        def unit_sem(yy, zz):
            return unit_recv.at[yy * NZ + zz]

        @pl.when(root)
        def _():
            def send_piece(i, carry):
                yy = i // NZ
                zz = lax.rem(i, NZ)
                remote(
                    a_ref.at[pl.ds(start_row(yy, zz), PIECE), :], piece(x, yy, zz),
                    s1_send, s1_recv, device(x, yy, zz, c),
                ).start()
                return carry

            lax.fori_loop(1, NY * NZ, send_piece, 0)
            mine = pltpu.make_async_copy(
                a_ref.at[pl.ds(start_row(0, 0), PIECE), :], piece(x, 0, 0), local_sem
            )
            mine.start()
            mine.wait()

        chunk = PW // CHUNKS
        base = row * PW
        far_base = (wrap(xh + 1, 2) * 2 + c) * PW

        def send_far(i):
            remote(
                a_ref.at[pl.ds(i * chunk, chunk), :],
                own.at[pl.ds(base + i * chunk, chunk), :],
                e1_send, e1_recv.at[i], x_far,
            ).start()

        def pass_far(i):
            rows = own.at[pl.ds(far_base + i * chunk, chunk), :]
            remote(rows, rows, e1_send, e1_recv.at[i], x_far).wait_recv()
            remote(rows, rows, e3_send, e3_recv.at[i], mate).start()

        def far_item(i):
            rows = own.at[pl.ds((wrap(xh + 1, 2) * 2 + 1 - c) * PW + i * chunk, chunk), :]
            remote(rows, rows, e3_send, e3_recv.at[i], mate).wait_recv()
            own_item(wrap(xh + 1, 2), i)

        send_far(0)
        near = remote(a_ref, own.at[pl.ds(base, PW), :], e2_send, e2_recv, mate)
        near.start()
        keep = pltpu.make_async_copy(a_ref, own.at[pl.ds(base, PW), :], keep_sem)
        keep.start()
        keep.wait()
        near.wait()
        for i in range(CHUNKS):
            own_item(xh, i)

        @pl.when(jnp.logical_not(root))
        def _():
            remote(piece(x, y, z), piece(x, y, z), s1_send, s1_recv, mate).wait_recv()

        for d in (1, 3, 2):
            remote(
                piece(x, y, z), piece(x, y, z), sx_send, sx_recv.at[d - 1],
                device(wrap(x + d, NX), y, z, c),
            ).start()
        for i in range(1, CHUNKS):
            send_far(i)
        pass_far(0)
        for d in (1, 3, 2):
            got = piece(wrap(x - d, NX), y, z)
            remote(got, got, sx_send, sx_recv.at[d - 1], mate).wait_recv()

        def send_z(yy, zz, d):
            remote(
                unit(yy, zz), unit(yy, zz), sz_send, unit_sem(yy, zz), device(x, y, wrap(z + d, NZ), c)
            ).start()

        def send_y(ref, yy, zz, d):
            remote(ref, ref, sy_send, unit_sem(yy, zz), device(x, wrap(y + d, NY), z, c)).start()

        def send_mate(yy, zz, s):
            remote(unit(yy, zz), unit(yy, zz), swap_send, swap_recv.at[s], mate).start()

        def arrived(yy, zz):
            remote(unit(yy, zz), unit(yy, zz), sz_send, unit_sem(yy, zz), mate).wait_recv()

        def swapped_in(s):
            ref = pan.at[1 - c, :, pl.ds(0, 64 * len(level(s))), :]
            remote(ref, ref, swap_send, swap_recv.at[s], mate).wait_recv()

        def items(s):
            return [functools.partial(panel_item, zz, b) for zz in level(s) for b in (0, 1)]

        if c == 0:
            def both_ways(zz, s):
                send_y(unit(y, zz), y, zz, 1)
                send_y(unit(y, zz), y, zz, -1)
                send_mate(y, zz, s)

            send_z(y, z, 1)
            send_z(y, z, -1)
            both_ways(z, 0)
            for s in range(1, 7):
                work = []
                if s >= 3:
                    swapped_in(s - 3)
                    work = items(s - 3)
                if s <= 4:
                    zz = wrap(z - s, NZ)
                    arrived(y, zz)
                    if s < 4:
                        send_z(y, zz, 1)
                    both_ways(zz, s)
                if s < 4:
                    zz = wrap(z + s, NZ)
                    arrived(y, zz)
                    if s < 3:
                        send_z(y, zz, -1)
                    both_ways(zz, s)
                for item in work[:1]:
                    item()
                if s - 1 <= 4:
                    for zz in level(s - 1):
                        yy = wrap(y - 1, NY)
                        arrived(yy, zz)
                        send_y(half_unit(yy, zz, 0), yy, zz, 1)
                        send_mate(yy, zz, s - 1)
                        yy = wrap(y + 1, NY)
                        arrived(yy, zz)
                        send_y(half_unit(yy, zz, 1), yy, zz, -1)
                        send_mate(yy, zz, s - 1)
                for item in work[1:3]:
                    item()
                if s >= 2:
                    for zz in level(s - 2):
                        yy = wrap(y + 2, NY)
                        arrived(yy, zz)
                        send_mate(yy, zz, s - 2)
                for item in work[3:]:
                    item()
                if s == 1:
                    far_item(0)
                if s in (2, 3, 4):
                    pass_far(s - 1)
                if s in (3, 4, 5):
                    far_item(s - 2)
            z_units, y_units = 7, 24
        else:
            for d in (1, 3, 2):
                send_y(unit(y, z), y, z, d)
            order = [y] + [wrap(y + d, NY) for d in (1, 3, 2)]
            for yy in order:
                if yy is not y:
                    arrived(yy, z)
                send_z(yy, z, 1)
                send_z(yy, z, -1)
                send_mate(yy, z, 0)
            for s in (1, 2, 3, 4):
                work = []
                if s >= 2:
                    work = items(s - 2)
                for k, yy in enumerate(order):
                    if s < 4 or k < 2:
                        zz = wrap(z - s, NZ)
                        arrived(yy, zz)
                        if s < 3 or (s == 3 and k < 2):
                            send_z(yy, zz, 1)
                        send_mate(yy, zz, s)
                    if s < 4 or k >= 2:
                        zz = wrap(z + s, NZ)
                        arrived(yy, zz)
                        if s < 3 or (s == 3 and k >= 2):
                            send_z(yy, zz, -1)
                        send_mate(yy, zz, s)
                    if k == 0 and work:
                        swapped_in(s - 2)
                    for item in work[k:k + 1]:
                        item()
                if s == 1:
                    far_item(0)
                if s in (2, 3, 4):
                    pass_far(s - 1)
                if s in (3, 4):
                    far_item(s - 2)
            swapped_in(3)
            for item in items(3):
                item()
            far_item(3)
            z_units, y_units = 28, 3

        def whole(send, recv, ref):
            return remote(ref, ref, send, recv, mate)

        swapped_in(4)
        block = own.at[pl.ds(0, PW), :]
        whole(sz_send, s1_recv, pan.at[c, :, pl.ds(0, PIECE * z_units), :]).wait_send()
        whole(sy_send, s1_recv, pan.at[c, :, pl.ds(0, PIECE * y_units), :]).wait_send()
        whole(sx_send, s1_recv, pan.at[c, pl.ds(0, 3), pl.ds(0, PIECE), :]).wait_send()
        whole(swap_send, s1_recv, pan.at[c]).wait_send()
        whole(e1_send, s1_recv, block).wait_send()
        whole(e3_send, s1_recv, block).wait_send()

        @pl.when(root)
        def _():
            rest = pan.at[c, 0, pl.ds(0, PIECE * (NY * NZ - 1)), :]
            whole(s1_send, s1_recv, rest).wait_send()

    for load in loads:
        load.wait()
    for i in range(4):
        high_parts[i], low_parts[i] = split(inverses[i // 2, i % 2])

    def inverse(i):
        return high_parts[i], low_parts[i]

    lower0, lower1, upper0, upper1 = [functools.partial(inverse, i) for i in range(4)]

    for c in (0, 1):
        pl.when(core == c)(functools.partial(run, c))

    for b in (0, 1):
        panel_item(level(4)[0], b)

    def put(condition, value):
        @pl.when(condition)
        def _():
            o_ref[...] = value

    put((row == 0) & (col == 0), acc[OWN_0])
    upper_rows = dot3(lower0(), split(acc[OWN_0]))
    put((row == 0) & (col > 0), upper_rows)
    top = split(upper_rows)
    lower_cols = dot3(split(acc[PANEL_0_1]), upper0())
    put((row == 1) & (col == 0), lower_cols)
    middle = acc[OWN_1] - dot3(split(lower_cols), top)
    put((row == 1) & (col == 1), middle)
    middle = dot3(lower1(), split(middle))
    put((row == 1) & (col > 1), middle)
    lower_cols = dot3(split(acc[PANEL_0_R]), upper0())
    put((row > 1) & (col == 0), lower_cols)
    lower_cols = split(lower_cols)
    rest = acc[OWN_R] - dot3(lower_cols, top)
    panel_top = dot3(lower0(), split(acc[PANEL_1_0]))
    lower_cols = acc[PANEL_1_R] - dot3(lower_cols, split(panel_top))
    lower_cols = dot3(split(lower_cols), upper1())
    put((row > 1) & (col == 1), lower_cols)
    put((row > 1) & (col > 1), rest - dot3(split(lower_cols), split(middle)))


def local(matrix, lower_inverses, upper_inverses, pivots):
    vmem = pl.BlockSpec(memory_space=pltpu.VMEM)
    dma = pltpu.SemaphoreType.DMA
    anywhere = pl.BlockSpec(memory_space=pl.ANY)
    return pl.pallas_call(
        kernel,
        out_shape=jax.ShapeDtypeStruct((PW, PW), F32),
        in_specs=[anywhere, anywhere, anywhere, vmem],
        out_specs=vmem,
        scratch_shapes=[
            pltpu.VMEM((2, NX, PW, PW), F32),
            pltpu.VMEM((4 * PW, PW), F32),
            pltpu.VMEM((7, PW, PW), F32),
            pltpu.VMEM((2, 2, PW, PW), F32),
            pltpu.VMEM((4, PW, PW), BF16),
            pltpu.VMEM((4, PW, PW), BF16),
            pltpu.VMEM((3, PW, LANES), F32),
            dma, dma, dma, dma((3,)), dma, dma, dma((NY * NZ,)), dma, dma((5,)),
            dma, dma((CHUNKS,)), dma, dma, dma, dma((CHUNKS,)), dma, dma, dma((2,)),
        ],
        compiler_params=pltpu.CompilerParams(
            collective_id=0, has_side_effects=True, vmem_limit_bytes=56 * 2**20
        ),
        name="panels",
    )(matrix, lower_inverses, upper_inverses, pivots)


def solution(mesh):
    return jax.shard_map(
        local,
        mesh=mesh,
        in_specs=(P("row", "col"), P(), P(), P()),
        out_specs=P("row", "col"),
        check_vma=False,
    )
```

time: 107 us -> 89 us (0.83)
  the two profiles are of different devices: /device:TPU:63 before, /device:TPU:5 now
where the time goes in v2:
time: 89 us; the launch traced here: 88.8 us
  Pallas kernels  86.5 us (97%)
  local copies, waits for them, and re-layouts  2.26 us (3%)
    pallas_call x1, Pallas kernels, local(): pl.pallas_call(kernel, out_shape=jax.ShapeDtypeStruct((PW, PW), F32), in_...  86.5 us
    unnamed x1, local copies, waits for them, and re-layouts  2.26 us

profile of v2, /device:TPU:5, one launch (start us, length us, event | category | flops | bytes accessed | tf_op | source)
XLA Modules:
  0.0 88.8 jit_solution(2847642431708599601)
XLA Ops:
  0.0 86.5 %panels.1 = f32[512,512]{1,0:T(8,128)} custom-call(f32[512,512]{1,0:T(8,128)} %a_ref.1, f32[2,512,512]{2,1,0:T(8,128)} %lower_ref.1, f32[2,512,512]{2,1,0:T(8,128)} %upper_ref.1, s32[2,512]{1,0:T(2,128)} %pivots_ref.1), custom_call_target="tpu_custom_call" | custom-call | tf_op jit(solution)/shard_map/panels/pallas_call | solution.py:406
  86.5 2.3 %copy.6 = f32[512,512]{1,0:T(8,128)} copy(f32[512,512]{1,0:T(8,128)} %panels.1) | data formatting | bytes 2097152

commit v3 on v0

v3 whole, which is shorter than its diff:
```python
import functools

import jax
import jax.numpy as jnp
from jax import lax
from jax.experimental import pallas as pl
from jax.experimental.pallas import tpu as pltpu
from jax.sharding import PartitionSpec as P

MESH = pl.DeviceIdType.MESH
PW = 512
NX, NY, NZ = 4, 4, 8
PIECE = 16
CHUNKS = 4
LANES = 128
LAG_1, LAG = 2, 4
OWN_0, OWN_1, OWN_R, PANEL_0_1, PANEL_0_R, PANEL_1_0, PANEL_1_R = range(7)
F32 = jnp.float32
BF16 = jnp.bfloat16


def split(value):
    high = value.astype(BF16)
    return high, (value - high.astype(F32)).astype(BF16)


def dot(a, b):
    return jnp.dot(a, b, preferred_element_type=F32)


def dot3(a, b):
    return dot(jnp.concatenate([a[0], a[0], a[1]], axis=1), jnp.concatenate([b[0], b[1], b[0]], axis=0))


def dot3_upper(a, b):
    h = PW // 2
    left = dot3([part[:, :h] for part in a], [part[:h, :h] for part in b])
    right = dot3(a, [part[:, h:] for part in b])
    return jnp.concatenate([left, right], axis=1)


def dot3_lower(a, b):
    h = PW // 2
    above = dot3([part[:h, :h] for part in a], [part[:h, :] for part in b])
    below = dot3([part[h:, :] for part in a], b)
    return jnp.concatenate([above, below], axis=0)


def device(x, y, z, core):
    return ((y * NZ + z) * 2 + lax.rem(x, 2), (x // 2) * 2 + core)


def wrap(value, size):
    return lax.rem(value + size, size)


def remote(src, dst, send, recv, target):
    return pltpu.make_async_remote_copy(
        src_ref=src, dst_ref=dst, send_sem=send, recv_sem=recv, device_id=target, device_id_type=MESH
    )


def column(row):
    shape = (PW, PW)
    eye = lax.broadcasted_iota(jnp.int32, shape, 0) == lax.broadcasted_iota(jnp.int32, shape, 1)
    return jnp.sum(jnp.where(eye, row, 0.0), axis=1, keepdims=True)


def swapped(rows, pivot_row, offset):
    lane = lax.broadcasted_iota(jnp.int32, (PW, PW), 1).astype(F32) + offset
    return rows + jnp.sum(jnp.where(pivot_row == rows, lane - rows, 0.0), axis=1, keepdims=True)


def kernel(
    a_ref, lower_ref, upper_ref, pivots_ref, o_ref,
    pan, own, acc, inverses, high_parts, low_parts, src,
    s1_send, s1_recv, sx_send, sx_recv, sz_send, sy_send, unit_recv, swap_send, swap_recv,
    e1_send, e1_recv, e2_send, e2_recv, e3_send, e3_recv, local_sem, keep_sem, inverse_sem,
):
    col = lax.axis_index("col")
    row = lax.axis_index("row")
    core = lax.rem(row, 2)
    xh = row // 2
    x = xh * 2 + lax.rem(col, 2)
    y = col // (2 * NZ)
    z = lax.rem(col // 2, NZ)
    root = (y == 0) & (z == 0)
    mate = device(x, y, z, 1 - core)
    x_far = device(wrap(x + 2, NX), y, z, core)

    partners = [mate]
    partners += [device(wrap(x + d, NX), y, z, core) for d in (1, 2, 3)]
    partners += [device(x, wrap(y + d, NY), z, core) for d in (1, 2, 3)]
    partners += [device(x, y, wrap(z + d, NZ), core) for d in (1, -1)]
    barrier = pltpu.get_barrier_semaphore()
    for partner in partners:
        pl.semaphore_signal(barrier, inc=1, device_id=partner, device_id_type=MESH)

    @pl.when(jnp.logical_not(root))
    def _():
        pl.semaphore_signal(barrier, inc=1, device_id=device(x, 0, 0, core), device_id_type=MESH)

    loads = [
        pltpu.make_async_copy(lower_ref, inverses.at[0], inverse_sem.at[0]),
        pltpu.make_async_copy(upper_ref, inverses.at[1], inverse_sem.at[1]),
    ]
    for load in loads:
        load.start()

    first = pivots_ref[0:1, :].astype(F32)
    second = pivots_ref[1:2, :].astype(F32)
    place = (lax.broadcasted_iota(jnp.int32, (PW, 1), 0) + row * PW).astype(F32)
    src[0] = jnp.broadcast_to(column(first), (PW, LANES))
    src[1] = jnp.broadcast_to(swapped(column(second), first, 0.0), (PW, LANES))
    src[2] = jnp.broadcast_to(swapped(swapped(place, second, float(PW)), first, 0.0), (PW, LANES))
    acc[...] = jnp.zeros(acc.shape, F32)

    @pl.when(jnp.logical_not(root))
    def _():
        pl.semaphore_wait(barrier, len(partners))

    @pl.when(root)
    def _():
        pl.semaphore_wait(barrier, len(partners) + NY * NZ - 1)

    def inverse(i):
        return high_parts[i], low_parts[i]

    lower0, lower1, upper0, upper1, top = [functools.partial(inverse, i) for i in range(5)]

    def put(condition, value):
        @pl.when(condition)
        def _():
            o_ref[...] = value

    def solve_top():
        value = dot3_lower(lower0(), split(acc[OWN_0]))
        put((row == 0) & (col == 0), acc[OWN_0])
        put((row == 0) & (col > 0), value)
        high_parts[4], low_parts[4] = split(value)

    lane = lax.broadcasted_iota(jnp.int32, (1, LANES), 1)

    def take(values, ids, targets):
        high, low = split(values)
        for which, dst in targets:
            pick = jnp.concatenate(
                [jnp.where(src[which] == part.astype(F32), 1.0, 0.0).astype(BF16) for part in ids], axis=1
            )
            acc[dst] += dot(jnp.concatenate([pick, pick], axis=1), jnp.concatenate([high, low], axis=0))

    def own_item(half, i):
        start = half * 2 * PW + i * LANES
        starts = [pl.multiple_of(start + j * PW, LANES) for j in (0, 1)]
        values = jnp.concatenate([own[pl.ds(at, LANES), :] for at in starts], axis=0)
        take(values, [lane + at for at in starts], [(0, OWN_0), (1, OWN_1), (2, OWN_R)])

    def panel_item(zz, b):
        rows = [pl.multiple_of(yy * LANES + zz * PIECE, PIECE) for yy in range(NY)]
        parts = [pan[0, 2 * q + b, pl.ds(at, PIECE), :] for q in (0, 1) for at in rows]
        at = pl.multiple_of(zz * 64, 64)
        parts += [pan[1, 2 * q + b, pl.ds(at, 64), :] for q in (0, 1)]
        within = lax.rem(lane, 64)
        high = (lane // 64) * (2 * PW)
        ids = [
            high + (within // PIECE) * LANES + lax.rem(within, PIECE) + zz * PIECE,
            high + PW + within + zz * 64,
        ]
        targets = [(2, PANEL_0_R), (1, PANEL_0_1)] if b == 0 else [(2, PANEL_1_R), (0, PANEL_1_0)]
        values = jnp.concatenate(parts, axis=0)
        if b == 0:
            values = dot3_upper(split(values), upper0())
        take(values, ids, targets)

    def nth(j):
        return wrap(z + (1 - 2 * lax.rem(j, 2)) * ((j + 1) // 2), NZ)

    def start_row(yy, zz, c):
        return pl.multiple_of(PIECE * ((yy * NZ + zz) * (1 - c) + (zz * NY + yy) * c), PIECE)

    def unit(yy, zz, c):
        return pan.at[c, :, pl.ds(start_row(yy, zz, c), PIECE), :]

    def half_unit(yy, zz, h, c):
        return pan.at[c, pl.ds(2 * h, 2), pl.ds(start_row(yy, zz, c), PIECE), :]

    def piece(xx, yy, zz):
        return pan.at[core, xx, pl.ds(start_row(yy, zz, core), PIECE), :]

    def unit_sem(yy, zz):
        return unit_recv.at[yy * NZ + zz]

    @pl.when(root)
    def _():
        def send_piece(i, carry):
            yy = lax.rem(i, NY)
            zz = lax.rem(i // NY + 2 * yy, NZ)
            remote(
                a_ref.at[pl.ds(start_row(yy, zz, core), PIECE), :], piece(x, yy, zz),
                s1_send, s1_recv, device(x, yy, zz, core),
            ).start()
            return carry

        lax.fori_loop(1, NY * NZ, send_piece, 0)
        mine = pltpu.make_async_copy(
            a_ref.at[pl.ds(start_row(0, 0, core), PIECE), :], piece(x, 0, 0), local_sem
        )
        mine.start()
        mine.wait()

    chunk = PW // CHUNKS
    base = row * PW
    other = wrap(xh + 1, 2)

    def far_rows(c, i):
        return own.at[pl.ds(pl.multiple_of((other * 2 + c) * PW + i * chunk, chunk), chunk), :]

    def send_far(i):
        remote(
            a_ref.at[pl.ds(pl.multiple_of(i * chunk, chunk), chunk), :],
            own.at[pl.ds(pl.multiple_of(base + i * chunk, chunk), chunk), :],
            e1_send, e1_recv.at[i], x_far,
        ).start()

    def pass_far(i):
        rows = far_rows(core, i)
        remote(rows, rows, e1_send, e1_recv.at[i], x_far).wait_recv()
        remote(rows, rows, e3_send, e3_recv.at[i], mate).start()

    def far_item(i):
        rows = far_rows(1 - core, i)
        remote(rows, rows, e3_send, e3_recv.at[i], mate).wait_recv()
        own_item(other, i)

    send_far(0)
    near = remote(a_ref, own.at[pl.ds(base, PW), :], e2_send, e2_recv, mate)
    near.start()
    keep = pltpu.make_async_copy(a_ref, own.at[pl.ds(base, PW), :], keep_sem)
    keep.start()
    for load in loads:
        load.wait()
    for i in range(4):
        high_parts[i], low_parts[i] = split(inverses[i // 2, i % 2])
    keep.wait()
    near.wait()

    def near_item(i, carry):
        own_item(xh, i)
        return carry

    lax.fori_loop(0, CHUNKS, near_item, 0)

    @pl.when(jnp.logical_not(root))
    def _():
        remote(piece(x, y, z), piece(x, y, z), s1_send, s1_recv, mate).wait_recv()

    for d in (1, 3, 2):
        remote(
            piece(x, y, z), piece(x, y, z), sx_send, sx_recv.at[d - 1],
            device(wrap(x + d, NX), y, z, core),
        ).start()
    send_far(1)
    pass_far(0)
    for d in (1, 3, 2):
        got = piece(wrap(x - d, NX), y, z)
        remote(got, got, sx_send, sx_recv.at[d - 1], mate).wait_recv()

    def send_z(yy, zz, d, c):
        ref = unit(yy, zz, c)
        remote(ref, ref, sz_send, unit_sem(yy, zz), device(x, y, wrap(z + d, NZ), c)).start()

    def send_y(ref, yy, zz, d, c):
        remote(ref, ref, sy_send, unit_sem(yy, zz), device(x, wrap(y + d, NY), z, c)).start()

    def send_mate(yy, zz, j, c):
        ref = unit(yy, zz, c)
        remote(ref, ref, swap_send, swap_recv.at[j], mate).start()

    def arrived(yy, zz, c):
        ref = unit(yy, zz, c)
        remote(ref, ref, sz_send, unit_sem(yy, zz), mate).wait_recv()

    def both_ways(zz, j):
        send_y(unit(y, zz, 0), y, zz, 1, 0)
        send_y(unit(y, zz, 0), y, zz, -1, 0)
        send_mate(y, zz, j, 0)

    order = [(0, y)] + [(k + 1, wrap(y + d, NY)) for k, d in enumerate((1, 3, 2))]

    @pl.when(core == 0)
    def _():
        send_z(y, z, 1, 0)
        send_z(y, z, -1, 0)
        both_ways(z, 0)

    @pl.when(core == 1)
    def _():
        for d in (1, 3, 2):
            send_y(unit(y, z, 1), y, z, d, 1)
        for k, yy in order:
            if k > 0:
                arrived(yy, z, 1)
            send_z(yy, z, 1, 1)
            send_z(yy, z, -1, 1)
            send_mate(yy, z, 0, 1)

    def slot_core_0(t):
        @pl.when(t <= 7)
        def _():
            zz = nth(t)
            arrived(y, zz, 0)

            @pl.when((lax.rem(t, 2) == 1) & (t < 7))
            def _():
                send_z(y, zz, 1, 0)

            @pl.when((lax.rem(t, 2) == 0) & (t < 6))
            def _():
                send_z(y, zz, -1, 0)

            both_ways(zz, t)

        @pl.when((t >= LAG_1) & (t <= 7 + LAG_1))
        def _():
            zz = nth(t - LAG_1)
            yy = wrap(y - 1, NY)
            arrived(yy, zz, 0)
            send_y(half_unit(yy, zz, 0, 0), yy, zz, 1, 0)
            send_mate(yy, zz, t - LAG_1, 0)
            yy = wrap(y + 1, NY)
            arrived(yy, zz, 0)
            send_y(half_unit(yy, zz, 1, 0), yy, zz, -1, 0)
            send_mate(yy, zz, t - LAG_1, 0)

        @pl.when(t >= LAG)
        def _():
            zz = nth(t - LAG)
            yy = wrap(y + 2, NY)
            arrived(yy, zz, 0)
            send_mate(yy, zz, t - LAG, 0)

    def slot_core_1(t):
        zz = nth(t)
        up = lax.rem(t, 2) == 1
        for k, yy in order:
            arrived(yy, zz, 1)
            send_mate(yy, zz, t, 1)

            @pl.when(up & ((t < 5) | ((t == 5) & (k < 2))))
            def _():
                send_z(yy, zz, 1, 1)

            @pl.when(jnp.logical_not(up) & ((t < 6) | ((t == 6) & (k >= 2))))
            def _():
                send_z(yy, zz, -1, 1)

    def slot(t, carry):
        @pl.when(core == 0)
        def _():
            slot_core_0(t)

        @pl.when((core == 1) & (t <= 6))
        def _():
            slot_core_1(t)

        @pl.when((t == 2) | (t == 4))
        def _():
            send_far(t // 2 + 1)

        @pl.when((t == 5) | (t == 7) | (t == 9))
        def _():
            pass_far((t - 3) // 2)

        @pl.when(t == 11)
        def _():
            solve_top()

        @pl.when(t >= LAG)
        def _():
            j = t - LAG
            ref = pan.at[1 - core, :, pl.ds(0, 64), :]
            remote(ref, ref, swap_send, swap_recv.at[j], mate).wait_recv()
            for b in (0, 1):
                panel_item(nth(j), b)

        @pl.when((core == 1) & (t == 9))
        def _():
            slot_core_1(7)

        @pl.when((t == 4) | (t == 6) | (t == 8) | (t == 10))
        def _():
            far_item(t // 2 - 2)

        return carry

    lax.fori_loop(1, 8 + LAG, slot, 0)

    put((row == 1) & (col == 0), acc[PANEL_0_1])
    put((row > 1) & (col == 0), acc[PANEL_0_R])
    middle = acc[OWN_1] - dot3(split(acc[PANEL_0_1]), top())
    put((row == 1) & (col == 1), middle)
    middle = dot3_lower(lower1(), split(middle))
    put((row == 1) & (col > 1), middle)
    lower_cols = split(acc[PANEL_0_R])
    rest = acc[OWN_R] - dot3(lower_cols, top())
    panel_top = dot3_lower(lower0(), split(acc[PANEL_1_0]))
    lower_cols = acc[PANEL_1_R] - dot3(lower_cols, split(panel_top))
    lower_cols = dot3_upper(split(lower_cols), upper1())
    put((row > 1) & (col == 1), lower_cols)
    put((row > 1) & (col > 1), rest - dot3(split(lower_cols), split(middle)))

    def sent(sem, ref):
        remote(ref, ref, sem, s1_recv, mate).wait_send()

    block = own.at[pl.ds(0, PW), :]
    sent(sx_send, pan.at[0, pl.ds(0, 3), pl.ds(0, PIECE), :])
    sent(swap_send, pan.at[0])
    sent(e1_send, block)
    sent(e3_send, block)

    @pl.when(core == 0)
    def _():
        sent(sz_send, pan.at[0, :, pl.ds(0, PIECE * 7), :])
        sent(sy_send, pan.at[0, :, pl.ds(0, PIECE * 24), :])

    @pl.when(core == 1)
    def _():
        sent(sz_send, pan.at[1, :, pl.ds(0, PIECE * 28), :])
        sent(sy_send, pan.at[1, :, pl.ds(0, PIECE * 3), :])

    @pl.when(root)
    def _():
        sent(s1_send, pan.at[0, 0, pl.ds(0, PIECE * (NY * NZ - 1)), :])


def local(matrix, lower_inverses, upper_inverses, pivots):
    vmem = pl.BlockSpec(memory_space=pltpu.VMEM)
    dma = pltpu.SemaphoreType.DMA
    anywhere = pl.BlockSpec(memory_space=pl.ANY)
    return pl.pallas_call(
        kernel,
        out_shape=pltpu.VMEM((PW, PW), F32),
        in_specs=[anywhere, anywhere, anywhere, vmem],
        out_specs=vmem,
        scratch_shapes=[
            pltpu.VMEM((2, NX, PW, PW), F32),
            pltpu.VMEM((4 * PW, PW), F32),
            pltpu.VMEM((7, PW, PW), F32),
            pltpu.VMEM((2, 2, PW, PW), F32),
            pltpu.VMEM((5, PW, PW), BF16),
            pltpu.VMEM((5, PW, PW), BF16),
            pltpu.VMEM((3, PW, LANES), F32),
            dma, dma, dma, dma((3,)), dma, dma, dma((NY * NZ,)), dma, dma((NZ,)),
            dma, dma((CHUNKS,)), dma, dma, dma, dma((CHUNKS,)), dma, dma, dma((2,)),
        ],
        compiler_params=pltpu.CompilerParams(
            collective_id=0, has_side_effects=True, vmem_limit_bytes=56 * 2**20
        ),
        name="panels",
    )(matrix, lower_inverses, upper_inverses, pivots)


def solution(mesh):
    return jax.shard_map(
        local,
        mesh=mesh,
        in_specs=(P("row", "col"), P(), P(), P()),
        out_specs=P("row", "col"),
        check_vma=False,
    )
```

time: 1400 us -> 77.1 us (0.06)
  the two profiles are of different devices: /device:TPU:4 before, /device:TPU:1 now
where the time goes in v3:
time: 77.1 us; the launch traced here: 76.9 us
  Pallas kernels  75.9 us (98%)
  local copies, waits for them, and re-layouts  0.97 us (1%)
    pallas_call x1, Pallas kernels, local(): pl.pallas_call(kernel, out_shape=pltpu.VMEM((PW, PW), F32), in_specs=[any...  75.9 us

profile of v3, /device:TPU:1, one launch (start us, length us, event | category | flops | bytes accessed | tf_op | source)
XLA Modules:
  0.0 76.9 jit_solution(184366428874798719)
XLA Ops:
  0.0 75.9 %panels.1 = f32[512,512]{1,0:T(8,128)S(1)} custom-call(f32[512,512]{1,0:T(8,128)} %a_ref.1, f32[2,512,512]{2,1,0:T(8,128)} %lower_ref.1, f32[2,512,512]{2,1,0:T(8,128)} %upper_ref.1, s32[2,512]{1,0:T(2,128)} %pivots_ref.1), custom_call_target="tpu_custom_call" | custom-call | tf_op jit(solution)/shard_map/panels/pallas_call | solution.py:440
  75.9 1.0 %copy.6 = f32[512,512]{1,0:T(8,128)} copy(f32[512,512]{1,0:T(8,128)S(1)} %panels.1) | data formatting | bytes 2097152

commit v4 on v3

--- a/solution.py
+++ b/solution.py
@@ -193,15 +193,16 @@
     @pl.when(root)
     def _():
         def send_piece(i, carry):
-            yy = lax.rem(i, NY)
-            zz = lax.rem(i // NY + 2 * yy, NZ)
+            yy = lax.rem(i + 1, NY)
+            k = i // NY
+            zz = lax.rem(NZ + NZ // 2 + (1 - 2 * lax.rem(k, 2)) * ((k + 1) // 2), NZ)
             remote(
                 a_ref.at[pl.ds(start_row(yy, zz, core), PIECE), :], piece(x, yy, zz),
                 s1_send, s1_recv, device(x, yy, zz, core),
             ).start()
             return carry
 
-        lax.fori_loop(1, NY * NZ, send_piece, 0)
+        lax.fori_loop(0, NY * NZ - 1, send_piece, 0)
         mine = pltpu.make_async_copy(
             a_ref.at[pl.ds(start_row(0, 0, core), PIECE), :], piece(x, 0, 0), local_sem
         )
@@ -295,11 +296,13 @@
 
     @pl.when(core == 1)
     def _():
+        send_z(y, z, 1, 1)
+        send_z(y, z, -1, 1)
         for d in (1, 3, 2):
             send_y(unit(y, z, 1), y, z, d, 1)
-        for k, yy in order:
-            if k > 0:
-                arrived(yy, z, 1)
+        send_mate(y, z, 0, 1)
+        for k, yy in order[1:]:
+            arrived(yy, z, 1)
             send_z(yy, z, 1, 1)
             send_z(yy, z, -1, 1)
             send_mate(yy, z, 0, 1)
@@ -359,10 +362,19 @@
         def _():
             slot_core_0(t)
 
-        @pl.when((core == 1) & (t <= 6))
+        @pl.when((core == 1) & (t <= 2))
         def _():
             slot_core_1(t)
 
+        @pl.when((core == 1) & ((t == 5) | (t == 7)))
+        def _():
+            slot_core_1(t - 2)
+            slot_core_1(t - 1)
+
+        @pl.when((core == 1) & (t == 10))
+        def _():
+            slot_core_1(7)
+
         @pl.when((t == 2) | (t == 4))
         def _():
             send_far(t // 2 + 1)
@@ -370,10 +382,6 @@
         @pl.when((t == 5) | (t == 7) | (t == 9))
         def _():
             pass_far((t - 3) // 2)
-
-        @pl.when(t == 11)
-        def _():
-            solve_top()
 
         @pl.when(t >= LAG)
         def _():
@@ -383,13 +391,13 @@
             for b in (0, 1):
                 panel_item(nth(j), b)
 
-        @pl.when((core == 1) & (t == 9))
-        def _():
-            slot_core_1(7)
-
-        @pl.when((t == 4) | (t == 6) | (t == 8) | (t == 10))
-        def _():
-            far_item(t // 2 - 2)
+        @pl.when((t == 3) | (t == 6) | (t == 8) | (t == 10))
+        def _():
+            far_item((t - 1) // 2 - 1)
+
+        @pl.when(t == 10)
+        def _():
+            solve_top()
 
         return carry
 

time: 77.1 us -> 73.8 us (0.957)
  the two profiles are of different devices: /device:TPU:1 before, /device:TPU:57 now
where the time goes in v4:
time: 73.8 us; the launch traced here: 73.6 us
  Pallas kernels  72.7 us (99%)
  local copies, waits for them, and re-layouts  0.97 us (1%)
    pallas_call x1, Pallas kernels, local(): pl.pallas_call(kernel, out_shape=pltpu.VMEM((PW, PW), F32), in_specs=[any...  72.7 us

profile of v4, /device:TPU:57, one launch (start us, length us, event | category | flops | bytes accessed | tf_op | source)
XLA Modules:
  0.0 73.6 jit_solution(15235279239220334856)
XLA Ops:
  0.0 72.7 %panels.1 = f32[512,512]{1,0:T(8,128)S(1)} custom-call(f32[512,512]{1,0:T(8,128)} %a_ref.1, f32[2,512,512]{2,1,0:T(8,128)} %lower_ref.1, f32[2,512,512]{2,1,0:T(8,128)} %upper_ref.1, s32[2,512]{1,0:T(2,128)} %pivots_ref.1), custom_call_target="tpu_custom_call" | custom-call | tf_op jit(solution)/shard_map/panels/pallas_call | solution.py:448
  72.7 1.0 %copy.6 = f32[512,512]{1,0:T(8,128)} copy(f32[512,512]{1,0:T(8,128)S(1)} %panels.1) | data formatting | bytes 2097152

commit v5 on v4

--- a/solution.py
+++ b/solution.py
@@ -107,14 +107,6 @@
     for load in loads:
         load.start()
 
-    first = pivots_ref[0:1, :].astype(F32)
-    second = pivots_ref[1:2, :].astype(F32)
-    place = (lax.broadcasted_iota(jnp.int32, (PW, 1), 0) + row * PW).astype(F32)
-    src[0] = jnp.broadcast_to(column(first), (PW, LANES))
-    src[1] = jnp.broadcast_to(swapped(column(second), first, 0.0), (PW, LANES))
-    src[2] = jnp.broadcast_to(swapped(swapped(place, second, float(PW)), first, 0.0), (PW, LANES))
-    acc[...] = jnp.zeros(acc.shape, F32)
-
     @pl.when(jnp.logical_not(root))
     def _():
         pl.semaphore_wait(barrier, len(partners))
@@ -238,6 +230,13 @@
     near.start()
     keep = pltpu.make_async_copy(a_ref, own.at[pl.ds(base, PW), :], keep_sem)
     keep.start()
+    first = pivots_ref[0:1, :].astype(F32)
+    second = pivots_ref[1:2, :].astype(F32)
+    place = (lax.broadcasted_iota(jnp.int32, (PW, 1), 0) + row * PW).astype(F32)
+    src[0] = jnp.broadcast_to(column(first), (PW, LANES))
+    src[1] = jnp.broadcast_to(swapped(column(second), first, 0.0), (PW, LANES))
+    src[2] = jnp.broadcast_to(swapped(swapped(place, second, float(PW)), first, 0.0), (PW, LANES))
+    acc[...] = jnp.zeros(acc.shape, F32)
     for load in loads:
         load.wait()
     for i in range(4):
@@ -255,7 +254,7 @@
     def _():
         remote(piece(x, y, z), piece(x, y, z), s1_send, s1_recv, mate).wait_recv()
 
-    for d in (1, 3, 2):
+    for d in (2, 1, 3):
         remote(
             piece(x, y, z), piece(x, y, z), sx_send, sx_recv.at[d - 1],
             device(wrap(x + d, NX), y, z, core),
@@ -371,7 +370,7 @@
             slot_core_1(t - 2)
             slot_core_1(t - 1)
 
-        @pl.when((core == 1) & (t == 10))
+        @pl.when((core == 1) & (t == 9))
         def _():
             slot_core_1(7)
 

time: 73.8 us -> 73.6 us (level)
  no operation moved by 1% of the time
where the time goes in v5:
time: 73.6 us; the launch traced here: 73.5 us
  Pallas kernels  72.5 us (99%)
  local copies, waits for them, and re-layouts  0.97 us (1%)
    pallas_call x1, Pallas kernels, local(): pl.pallas_call(kernel, out_shape=pltpu.VMEM((PW, PW), F32), in_specs=[any...  72.5 us

profile of v5, /device:TPU:57, one launch (start us, length us, event | category | flops | bytes accessed | tf_op | source)
XLA Modules:
  0.0 73.5 jit_solution(13454753269801074473)
XLA Ops:
  0.0 72.5 %panels.1 = f32[512,512]{1,0:T(8,128)S(1)} custom-call(f32[512,512]{1,0:T(8,128)} %a_ref.1, f32[2,512,512]{2,1,0:T(8,128)} %lower_ref.1, f32[2,512,512]{2,1,0:T(8,128)} %upper_ref.1, s32[2,512]{1,0:T(2,128)} %pivots_ref.1), custom_call_target="tpu_custom_call" | custom-call | tf_op jit(solution)/shard_map/panels/pallas_call | solution.py:447
  72.5 1.0 %copy.6 = f32[512,512]{1,0:T(8,128)} copy(f32[512,512]{1,0:T(8,128)S(1)} %panels.1) | data formatting | bytes 2097152
